TPU v7x, 32 devices: a whole 2x2x4 slice. The times are simulated.
32 devices in a mesh: tm: 4 (over y, x), slab: 8 (over z, core).
Axes of the slice: x: 2, y: 2, z: 4, core: 2. Of those that a mesh axis runs over, the one named last changes fastest.
Arguments:
- u_states: bfloat16 [4, 64, 32, 8, 256], P('tm', None, 'slab'), may hold values from -6 to 6
- lam_points: float32 [4, 64, 32, 8, 256], P('tm', None, 'slab'), may hold values from -6 to 6
- weight: bfloat16 [27, 64, 64], replicated, may hold values from -0.15625 to 0.15625
- bias: float32 [64], replicated, may hold values from -3 to 3
Outputs:
- lam_new: float32 [4, 64, 32, 8, 256], P('tm', None, 'slab')
- grad_w: float32 [27, 64, 64], replicated
- grad_b: float32 [64], replicated
All inputs are finite; a program needn't handle non-finite values.
Results may differ from a plain program's by a relative error of at most 0.0065.
Values may be sent and summed in bfloat16 or wider, within the bound.
A program may use at most 256 MiB of HBM per device.

v0:
```python
import math

import jax
import jax.numpy as jnp
from jax import lax
from jax.sharding import PartitionSpec as P

step_size = 0.25


def padded_2(x, sides, width):
    for axis, dim in sides:
        devices, length = (lax.axis_size(axis), x.shape[dim])
        up = [(i, (i + 1) % devices) for i in range(devices - 1)]
        down = [(j, i) for i, j in up]
        last = lax.slice_in_dim(x, length - width, length, axis=dim)
        initial = lax.slice_in_dim(x, 0, width, axis=dim)
        before = lax.ppermute(last, axis, up)
        after = lax.ppermute(initial, axis, down)
        x = jnp.concatenate([before, x, after], axis=dim)
    return x


def passed_along(value, axis, steps):
    count = lax.axis_size(axis)
    initial, last = (max(0, -steps), min(count, count - steps))
    return lax.ppermute(value, axis, [(source, source + steps) for source in range(initial, last)])


def columns(widened, z_shift, x_shift, planes):
    channels = widened.shape[0]
    extent_x = widened.shape[2] - 2
    extent_y = widened.shape[3] - 2
    shifted = [
        widened[
            :,
            z_shift : z_shift + planes,
            x_shift : x_shift + extent_x,
            y_shift : y_shift + extent_y,
        ]
        for y_shift in range(3)
    ]
    return jnp.concatenate(shifted, 0).reshape(3 * channels, planes * extent_x * extent_y)


def apply_taps(padded, taps):
    widened = jnp.pad(padded, ((0, 0), (0, 0), (1, 1), (1, 1)))
    planes = padded.shape[1] - 2
    outputs = taps.shape[1]
    running = jnp.zeros((outputs, planes * padded.shape[2] * padded.shape[3]), jnp.float32)
    for z_shift in range(3):
        for x_shift in range(3):
            first_tap = 9 * z_shift + 3 * x_shift
            matrix = (
                taps[first_tap : first_tap + 3]
                .transpose(1, 0, 2)
                .reshape(outputs, 3 * taps.shape[2])
            )
            running = running + jnp.dot(
                matrix,
                columns(widened, z_shift, x_shift, planes),
                preferred_element_type=jnp.float32,
            )
    return running.reshape(outputs, planes, padded.shape[2], padded.shape[3])


def taps_grad(cotangent, padded):
    widened = jnp.pad(padded, ((0, 0), (0, 0), (1, 1), (1, 1)))
    planes = cotangent.shape[1]
    channels = cotangent.shape[0]
    flattened = cotangent.reshape(channels, -1)
    blocks = []
    for z_shift in range(3):
        for x_shift in range(3):
            product = lax.dot_general(
                flattened,
                columns(widened, z_shift, x_shift, planes),
                (((1,), (1,)), ((), ())),
                preferred_element_type=jnp.float32,
            )
            blocks.append(product.reshape(channels, 3, padded.shape[0]).transpose(1, 0, 2))
    return jnp.concatenate(blocks, 0)


def restrict(field):
    shaped = field.reshape(
        field.shape[0], field.shape[1], field.shape[2] // 2, 2, field.shape[3] // 2, 2
    )
    return jnp.mean(shaped, axis=(3, 5))


def prolong(field):
    return jnp.repeat(jnp.repeat(field, 2, axis=2), 2, axis=3)


def transposed(cotangent, flipped):
    padded = padded_2(cotangent, (("slab", 1),), 1)
    return apply_taps(padded, flipped)


def on_device(u_states, lam_points, weight, bias):
    state_zero = u_states[0]
    adjoint = lam_points[0]
    depth_cells = state_zero.shape[1]
    offset = bias[:, None, None, None]
    flipped = weight[::-1].transpose(0, 2, 1)
    zero_pad = padded_2(state_zero, (("slab", 1),), 1)
    tanh_zero = jnp.tanh(apply_taps(zero_pad, weight) + offset)
    state_one = (state_zero.astype(jnp.float32) + step_size * tanh_zero).astype(jnp.bfloat16)
    one_pad = padded_2(state_one, (("slab", 1),), 1)
    sens_zero = 1.0 - tanh_zero * tanh_zero
    tanh_one = jnp.tanh(apply_taps(one_pad, weight) + offset)
    sens_one = 1.0 - tanh_one * tanh_one
    cot_one = (sens_one * adjoint).astype(jnp.bfloat16)
    middle = adjoint + step_size * transposed(cot_one, flipped)
    cot_zero = (sens_zero * middle).astype(jnp.bfloat16)
    fine_back = middle + step_size * transposed(cot_zero, flipped)
    weight_grad = taps_grad(cot_zero, zero_pad) + taps_grad(cot_one, one_pad)
    bias_grad = jnp.sum(cot_zero.astype(jnp.float32) + cot_one.astype(jnp.float32), axis=(1, 2, 3))
    diagonal = jnp.diagonal(weight[13]).astype(jnp.float32)
    factor = 1.0 + 2.0 * step_size * diagonal[:, None, None, None] * restrict(sens_zero)
    lower, factor_prev = passed_along((restrict(fine_back), factor), "tm", 1)
    rest = lower - restrict(adjoint)

    def sweep_once(counter, value):
        return factor_prev * passed_along(value, "tm", 1) + rest

    correction = lax.fori_loop(0, lax.axis_size("tm") - 1, sweep_once, rest)
    updated = adjoint + prolong(correction)
    weight_total, bias_total = lax.psum((weight_grad, bias_grad), ("tm", "slab"))
    grad_scale = step_size / math.sqrt(
        2
        * lax.axis_size("tm")
        * depth_cells
        * lax.axis_size("slab")
        * state_zero.shape[2]
        * state_zero.shape[3]
    )
    return (updated[None], weight_total * grad_scale, bias_total * grad_scale)


def solution(mesh):
    in_specs = (P("tm", None, "slab", None, None), P("tm", None, "slab", None, None), P(), P())
    out_specs = (P("tm", None, "slab", None, None), P(), P())
    return jax.shard_map(
        on_device, mesh=mesh, in_specs=in_specs, out_specs=out_specs, check_vma=False
    )
```

profile of v0, /device:TPU:4, one launch (start us, length us, event | category | flops | bytes accessed | tf_op | source)
XLA Modules:
  0.0 677.0 jit_solution(8367435631987069173)
XLA Ops:
  13.2 2.4 concatenate.188
  18.0 5.0 fusion.21
  22.9 9.0 %fusion.96 = (bf16[64,4,8,256]{3,2,1,0:T(8,128)(2,1)S(1)}, bf16[64,4,8,256]{3,2,1,0:T(8,128)(2,1)S(1)}, bf16[64,4,8,256]{3,2,1,0:T(8,128)(2,1)S(1)}, bf16[64,4,8...) fusion(bf16[64,6,10,258]{3,2,1,0:T(8,128)(2,1)S(1)} %fusion.21), kind=kLoop, calls=%fused_computation.218 | loop fusion | bytes 39845888 | tf_op jit(solution)/shard_map/slice | solution.py:35
  31.9 3.7 fusion.97
  35.6 3.5 pad_maximum_fusion.35
  59.5 2.3 copy.95
  73.4 10.9 %convolution_add_fusion.28 = f32[8192,64]{0,1:T(8,128)S(1)} fusion(f32[8192,64]{0,1:T(8,128)S(1)} %convolution_add_fusion.29, bf16[64,192]{0,1:T(8,128)(2,1)S(1)} %bitcast.599, bf16[64,8192]{1,0:T(8,128)(2,1)S(1)} %bitcast.564, bf16[64,8192]{1,0:T(8,128)(2,1)S(1)} %copy-done.89, bf16[64,8192]{1,0:T(8,128)(2,1)S(1)} %bitcast.563), kind=kOutput, calls=%fused_computation.40 | convolution fusion | flops 211288064 | bytes 7364608 | tf_op jit(solution)/shard_map/dot_general | solution.py:59
  91.8 4.4 collective-permute-start.3
  99.1 2.8 copy.64
  101.9 3.3 copy.86
  106.0 3.8 copy.78
  109.8 6.8 %copy.79 = f32[64,4,4,2,128,2]{4,0,5,3,2,1:T(8,128)} copy(f32[64,4,4,2,128,2]{0,5,4,3,2,1:T(2,128)} %bitcast.536) | data formatting | bytes 4194304 | tf_op jit(solution)/shard_map/reshape | solution.py:64
  116.5 5.8 fusion.19
  122.4 8.9 %fusion.94 = (bf16[64,4,8,256]{3,2,1,0:T(8,128)(2,1)S(1)}, bf16[64,4,8,256]{3,2,1,0:T(8,128)(2,1)S(1)}, bf16[64,4,8,256]{3,2,1,0:T(8,128)(2,1)S(1)}, bf16[64,4,8...) fusion(bf16[64,6,10,258]{3,2,1,0:T(8,128)(2,1)S(1)} %fusion.19), kind=kLoop, calls=%fused_computation.216 | loop fusion | bytes 39845888 | tf_op jit(solution)/shard_map/slice | solution.py:35
  131.3 3.6 fusion.95
  144.1 4.0 copy.103
  148.5 3.9 copy.102
  152.5 4.5 fusion.31
  182.3 4.4 collective-permute-start.5
  189.3 3.4 dot_general.282
  192.7 5.9 dot_general.284
  198.6 6.1 dot_general.286
  204.7 3.5 dot_general.288
  208.1 6.0 dot_general.292
  214.1 3.4 dot_general.294
  217.5 6.0 dot_general.296
  223.6 3.4 dot_general.298
  227.0 6.0 dot_general.290
  235.0 3.4 collective-permute-start.10
  238.4 3.5 dot_general.300
  241.8 5.9 dot_general.302
  247.7 6.0 dot_general.304
  253.7 3.5 dot_general.306
  257.2 5.9 dot_general.308
  263.0 6.0 dot_general.310
  269.1 3.4 dot_general.312
  272.5 6.0 dot_general.314
  278.5 3.4 dot_general.316
  282.7 9.3 %select_maximum_fusion.2 = bf16[64,6,10,258]{3,2,1,0:T(8,128)(2,1)S(1)} fusion(bf16[64,1,8,256]{3,2,1,0:T(8,128)(2,1)} %collective-permute-done.6, bf16[64,4,8,256]{3,2,1,0:T(8,128)(2,1)} %copy-done.40, bf16[64,1,8,256]{3,2,1,0:T(8,128)(2,1)S(1)} %collective-permute-done.5), kind=kLoop, calls=%fused_computation.46 | loop fusion | flops 18823680 | bytes 3554304 | tf_op jit(solution)/shard_map/concatenate | solution.py:20
  292.0 8.9 %fusion.92 = (bf16[64,4,8,256]{3,2,1,0:T(8,128)(2,1)S(1)}, bf16[64,4,8,256]{3,2,1,0:T(8,128)(2,1)S(1)}, bf16[64,4,8,256]{3,2,1,0:T(8,128)(2,1)S(1)}, bf16[64,4,8...) fusion(bf16[64,6,10,258]{3,2,1,0:T(8,128)(2,1)S(1)} %select_max, ...), kind=kLoop, calls=%fused_computation.214 | loop fusion | bytes 39845888 | tf_op jit(solution)/shard_map/slice | solution.py:35
  300.9 3.5 fusion.93
  317.8 4.7 fusion.27
  322.5 4.3 copy.111
  342.8 2.4 add_reduce_fusion.1
  349.6 4.0 collective-permute-start.7
  354.9 3.9 copy.74
  358.8 4.0 fusion.59
  394.4 5.8 select_maximum_fusion
  400.2 9.0 %fusion.90 = (bf16[64,4,8,256]{3,2,1,0:T(8,128)(2,1)S(1)}, bf16[64,4,8,256]{3,2,1,0:T(8,128)(2,1)S(1)}, bf16[64,4,8,256]{3,2,1,0:T(8,128)(2,1)S(1)}, bf16[64,4,8...) fusion(bf16[64,6,10,258]{3,2,1,0:T(8,128)(2,1)S(1)} %select_max, ...), kind=kLoop, calls=%fused_computation.212 | loop fusion | bytes 39845888 | tf_op jit(solution)/shard_map/slice | solution.py:35
  409.2 3.6 fusion.91
  426.2 5.1 fusion.23
  449.1 3.0 copy.75
  452.1 11.6 %fusion.88 = (f32[64,4,4,128]{0,3,2,1:T(8,128)S(1)}, f32[64,4,4,128]{0,3,2,1:T(8,128)S(1)}) fusion(f32[64,4,4,2,128,2]{0,5,4,3,2,1:T(2,128)} %bitcast.532, f32[64,4,4,2,128,2]{0,5,4,3,2,1:T(2,128)} %bitcast.534, f32[64,4,4,2,128,2]{0,5,4,3,2,1:T(2,128)} %bitcast.533), kind=kLoop, calls=%fused_computation.211 | loop fusion | flops 1835008 | bytes 7340032 | tf_op jit(solution)/shard_map/reduce_sum | solution.py:89
  466.8 3.9 fusion.60
  470.7 2.5 add.265
  474.7 45.5 %psum.15 = f32[64]{0:T(128)S(1)} all-reduce(f32[64]{0:T(128)S(1)} %copy-done.122), channel_id=1, replica_groups=mesh['tm'=4,'slab'=8] {'tm','slab'}, use_global_device_ids=true, to_apply=%region_7.8 | all-reduce | flops 64 | bytes 512 | tf_op jit(solution)/shard_map/psum | solution.py:130
  520.6 86.3 %all-reduce.6.cloned.1.call-done = f32[27,64,64]{2,1,0:T(8,128)} async-done(((f32[27,64,64]{2,1,0:T(8,128)}), f32[27,64,64]{2,1,0:T(8,128)}) %all-reduce.6.cloned.1.call-update) | async-done | bytes 442384 | tf_op jit(solution)/shard_map/psum | solution.py:130
  613.2 46.2 %while.10 = (s32[]{:T(128)}, f32[64,4,4,128]{3,2,1,0:T(4,128)S(1)}, f32[64,4,4,128]{3,2,1,0:T(4,128)S(1)}, f32[64,4,4,128]{3,2,1,0:T(4,128)S(1)}, s32[]{:T(128)}) while((s32[]{:T(128)}, f32[64,4,4,128]{3,2,1,0:T(4,128)S(1)}, f32[64,4,4,128]{3,2,1,0:T(4,128)S(1)}, f32[64,4,4,128]{3,2,1,0:T(4,128)S(1)}, s32[]{:T(128)}) %tuple.152), condition=%wide.region_4.5_spmd, body=%wide.region_3.4_spmd.sunk | while | flops 262146 | bytes 4194405 | solution.py:128
  613.3 3.3 collective-permute-start
  616.5 12.9 %collective-permute-done = f32[64,4,4,128]{3,2,1,0:T(4,128)S(1)} collective-permute-done((f32[64,4,4,128]{3,2,1,0:T(4,128)S(1)}, f32[64,4,4,128]{3,2,1,0:T(4,128)S(1)}, u32[]{:S(2)}, u32[]{:S(2)}) %collective-permute-start) | collective-permute-done | bytes 524320 | tf_op jit(solution)/shard_map/while/body/eval_jaxpr/ppermute | solution.py:27
  631.5 13.3 %collective-permute-done = f32[64,4,4,128]{3,2,1,0:T(4,128)S(1)} collective-permute-done((f32[64,4,4,128]{3,2,1,0:T(4,128)S(1)}, f32[64,4,4,128]{3,2,1,0:T(4,128)S(1)}, u32[]{:S(2)}, u32[]{:S(2)}) %collective-permute-start) | collective-permute-done | bytes 524320 | tf_op jit(solution)/shard_map/while/body/eval_jaxpr/ppermute | solution.py:27
  646.9 12.4 %collective-permute-done = f32[64,4,4,128]{3,2,1,0:T(4,128)S(1)} collective-permute-done((f32[64,4,4,128]{3,2,1,0:T(4,128)S(1)}, f32[64,4,4,128]{3,2,1,0:T(4,128)S(1)}, u32[]{:S(2)}, u32[]{:S(2)}) %collective-permute-start) | collective-permute-done | bytes 524320 | tf_op jit(solution)/shard_map/while/body/eval_jaxpr/ppermute | solution.py:27
  662.8 2.4 add.260
  665.2 4.5 copy.87
  (416 shorter events, 206.8 us)
Async XLA Ops:
  7.2 10.8 %copy-start.33 = (bf16[1,64,4,8,256]{4,3,2,1,0:T(8,128)(2,1)S(1)}, bf16[1,64,4,8,256]{4,3,2,1,0:T(8,128)(2,1)}, u32[]{:S(2)}) copy-start(bf16[1,64,4,8,256]{4,3,2,1,0:T(8,128)(2,1)} %param.6) | copy-start | bytes 3145732
  7.2 599.7 %all-reduce.6.cloned.1.call-start = ((), (), s32[]{:S(2)}) async-start(), calls=%async_computation | async-start | bytes 1769472 | tf_op jit(solution)/shard_map/psum | solution.py:130
  8.4 9.6 %collective-permute-start.1 = (bf16[64,1,8,256]{3,2,1,0:T(8,128)(2,1)S(1)}, bf16[64,1,8,256]{3,2,1,0:T(8,128)(2,1)S(1)}, u32[]{:S(2)}, u32[]{:S(2)}) collective-permute-start(bf16[64,1,8,256]{3,2,1,0:T(8,128)(2,1)S(1)} %get-tuple-element.177), channel_id=1, source_target_pairs={{0,1},{1,2},{2,3},{3,4},{4,5},{5,6},{6,7},{8,9},{9,10},{10,11},{11... | collective-permute-start | bytes 786440 | tf_op jit(solution)/shard_map/ppermute | solution.py:18
  10.1 7.8 %collective-permute-start.2 = (bf16[64,1,8,256]{3,2,1,0:T(8,128)(2,1)S(1)}, bf16[64,1,8,256]{3,2,1,0:T(8,128)(2,1)S(1)}, u32[]{:S(2)}, u32[]{:S(2)}) collective-permute-start(bf16[64,1,8,256]{3,2,1,0:T(8,128)(2,1)S(1)} %get-tuple-element.178), channel_id=1, source_target_pairs={{1,0},{2,1},{3,2},{4,3},{5,4},{6,5},{7,6},{9,8},{10,9},{11,10},{12... | collective-permute-start | bytes 786440 | tf_op jit(solution)/shard_map/ppermute | solution.py:19
  15.7 53.6 %copy-start.115 = (bf16[64,3,64]{0,2,1:T(8,128)(2,1)}, bf16[64,3,64]{0,2,1:T(8,128)(2,1)S(1)}, u32[]{:S(2)}) copy-start(bf16[64,3,64]{0,2,1:T(8,128)(2,1)S(1)} %copy.65) | copy-start | bytes 73732
  15.8 54.2 %copy-start.111 = (bf16[64,3,64]{0,2,1:T(8,128)(2,1)}, bf16[64,3,64]{0,2,1:T(8,128)(2,1)S(1)}, u32[]{:S(2)}) copy-start(bf16[64,3,64]{0,2,1:T(8,128)(2,1)S(1)} %copy.66) | copy-start | bytes 73732
  15.9 54.9 %copy-start.109 = (bf16[64,3,64]{0,2,1:T(8,128)(2,1)}, bf16[64,3,64]{0,2,1:T(8,128)(2,1)S(1)}, u32[]{:S(2)}) copy-start(bf16[64,3,64]{0,2,1:T(8,128)(2,1)S(1)} %copy.67) | copy-start | bytes 73732
  16.0 55.5 %copy-start.107 = (bf16[64,3,64]{0,2,1:T(8,128)(2,1)}, bf16[64,3,64]{0,2,1:T(8,128)(2,1)S(1)}, u32[]{:S(2)}) copy-start(bf16[64,3,64]{0,2,1:T(8,128)(2,1)S(1)} %copy.68) | copy-start | bytes 73732
  16.1 56.2 %copy-start.117 = (bf16[64,3,64]{0,2,1:T(8,128)(2,1)}, bf16[64,3,64]{0,2,1:T(8,128)(2,1)S(1)}, u32[]{:S(2)}) copy-start(bf16[64,3,64]{0,2,1:T(8,128)(2,1)S(1)} %copy.69) | copy-start | bytes 73732
  16.2 68.1 %copy-start.105 = (bf16[64,3,64]{0,2,1:T(8,128)(2,1)}, bf16[64,3,64]{0,2,1:T(8,128)(2,1)S(1)}, u32[]{:S(2)}) copy-start(bf16[64,3,64]{0,2,1:T(8,128)(2,1)S(1)} %copy.70) | copy-start | bytes 73732
  39.1 25.6 %copy-start.26 = (bf16[192,4,8,256]{3,2,1,0:T(8,128)(2,1)}, bf16[192,4,8,256]{3,2,1,0:T(8,128)(2,1)S(1)}, u32[]{:S(2)}) copy-start(bf16[192,4,8,256]{3,2,1,0:T(8,128)(2,1)S(1)} %get-tuple-element.160) | copy-start | bytes 9437188
  39.1 3.1 copy-start.68
  39.1 4.1 copy-start.69
  39.1 4.4 copy-start.70
  44.2 2.4 copy-start.18
  44.2 22.7 %copy-start.16 = (bf16[192,4,8,256]{3,2,1,0:T(8,128)(2,1)}, bf16[192,4,8,256]{3,2,1,0:T(8,128)(2,1)S(1)}, u32[]{:S(2)}) copy-start(bf16[192,4,8,256]{3,2,1,0:T(8,128)(2,1)S(1)} %get-tuple-element.199) | copy-start | bytes 9437188
  44.3 3.1 copy-start.65
  44.3 4.1 copy-start.66
  49.4 2.9 copy-start.20
  54.5 3.2 copy-start.63
  59.5 2.9 copy-start.23
  89.3 8.2 %copy-start.86 = (bf16[27,64,64]{2,1,0:T(8,128)(2,1)S(1)}, bf16[27,64,64]{2,1,0:T(8,128)(2,1)}, u32[]{:S(2)}) copy-start(bf16[27,64,64]{2,1,0:T(8,128)(2,1)} %param.8) | copy-start | bytes 663556
  89.3 8.2 %copy-start = (f32[1,64,4,8,256]{4,3,2,1,0:T(8,128)S(1)}, f32[1,64,4,8,256]{4,3,2,1,0:T(8,128)}, u32[]{:S(2)}) copy-start(f32[1,64,4,8,256]{4,3,2,1,0:T(8,128)} %param.7) | copy-start | bytes 6291460
  91.8 24.7 %collective-permute-start.3 = (bf16[64,1,8,256]{3,2,1,0:T(8,128)(2,1)}, bf16[64,1,8,256]{3,2,1,0:T(8,128)(2,1)S(1)}, u32[]{:S(2)}, u32[]{:S(2)}) collective-permute-start(bf16[64,1,8,256]{3,2,1,0:T(8,128)(2,1)} %get-tuple-element.175), channel_id=1, source_target_pairs={{0,1},{1,2},{2,3},{3,4},{4,5},{5,6},{6,7},{8,9},{9,10},{10,11},{11... | collective-permute-start | bytes 786440 | tf_op jit(solution)/shard_map/ppermute | solution.py:18
  96.2 20.3 %collective-permute-start.4 = (bf16[64,1,8,256]{3,2,1,0:T(8,128)(2,1)}, bf16[64,1,8,256]{3,2,1,0:T(8,128)(2,1)}, u32[]{:S(2)}, u32[]{:S(2)}) collective-permute-start(bf16[64,1,8,256]{3,2,1,0:T(8,128)(2,1)} %get-tuple-element.176), channel_id=1, source_target_pairs={{1,0},{2,1},{3,2},{4,3},{5,4},{6,5},{7,6},{9,8},{10,9},{11,10},{12... | collective-permute-start | bytes 786440 | tf_op jit(solution)/shard_map/ppermute | solution.py:19
  109.8 6.8 %copy-start.39 = (bf16[64,4,8,256]{3,2,1,0:T(8,128)(2,1)S(1)}, bf16[64,4,8,256]{3,2,1,0:T(8,128)(2,1)}, u32[]{:S(2)}) copy-start(bf16[64,4,8,256]{3,2,1,0:T(8,128)(2,1)} %copy-done.38) | copy-start | bytes 3145732
  141.0 2.7 copy-start.84
  144.1 4.0 copy-start.11
  148.5 4.0 copy-start.13
  156.9 7.1 %copy-start.30 = (bf16[192,4,8,256]{3,2,1,0:T(8,128)(2,1)}, bf16[192,4,8,256]{3,2,1,0:T(8,128)(2,1)S(1)}, u32[]{:S(2)}) copy-start(bf16[192,4,8,256]{3,2,1,0:T(8,128)(2,1)S(1)} %get-tuple-element.174) | copy-start | bytes 9437188
  156.9 7.8 %copy-start.29 = (bf16[192,4,8,256]{3,2,1,0:T(8,128)(2,1)}, bf16[192,4,8,256]{3,2,1,0:T(8,128)(2,1)S(1)}, u32[]{:S(2)}) copy-start(bf16[192,4,8,256]{3,2,1,0:T(8,128)(2,1)S(1)} %get-tuple-element.173) | copy-start | bytes 9437188
  156.9 10.1 %copy-start.28 = (bf16[192,4,8,256]{3,2,1,0:T(8,128)(2,1)}, bf16[192,4,8,256]{3,2,1,0:T(8,128)(2,1)S(1)}, u32[]{:S(2)}) copy-start(bf16[192,4,8,256]{3,2,1,0:T(8,128)(2,1)S(1)} %get-tuple-element.172) | copy-start | bytes 9437188
  157.0 3.1 copy-start.78
  157.0 4.2 copy-start.79
  180.0 8.0 %copy-start.62 = (f32[64,4,4,2,128,2]{4,0,5,3,2,1:T(8,128)S(1)}, f32[64,4,4,2,128,2]{4,0,5,3,2,1:T(8,128)}, u32[]{:S(2)}) copy-start(f32[64,4,4,2,128,2]{4,0,5,3,2,1:T(8,128)} %copy.79) | copy-start | bytes 6291460
  181.5 7.8 %copy-start.19 = (bf16[192,4,8,256]{3,2,1,0:T(8,128)(2,1)S(1)}, bf16[192,4,8,256]{3,2,1,0:T(8,128)(2,1)}, u32[]{:S(2)}) copy-start(bf16[192,4,8,256]{3,2,1,0:T(8,128)(2,1)} %copy-done.18) | copy-start | bytes 9437188
  182.3 99.6 %collective-permute-start.5 = (bf16[64,1,8,256]{3,2,1,0:T(8,128)(2,1)}, bf16[64,1,8,256]{3,2,1,0:T(8,128)(2,1)S(1)}, u32[]{:S(2)}, u32[]{:S(2)}) collective-permute-start(bf16[64,1,8,256]{3,2,1,0:T(8,128)(2,1)} %get-tuple-element.170), channel_id=1, source_target_pairs={{0,1},{1,2},{2,3},{3,4},{4,5},{5,6},{6,7},{8,9},{9,10},{10,11},{11... | collective-permute-start | bytes 786440 | tf_op jit(solution)/shard_map/ppermute | solution.py:18
  186.7 95.2 %collective-permute-start.6 = (bf16[64,1,8,256]{3,2,1,0:T(8,128)(2,1)}, bf16[64,1,8,256]{3,2,1,0:T(8,128)(2,1)}, u32[]{:S(2)}, u32[]{:S(2)}) collective-permute-start(bf16[64,1,8,256]{3,2,1,0:T(8,128)(2,1)} %get-tuple-element.171), channel_id=1, source_target_pairs={{1,0},{2,1},{3,2},{4,3},{5,4},{6,5},{7,6},{9,8},{10,9},{11,10},{12... | collective-permute-start | bytes 786440 | tf_op jit(solution)/shard_map/ppermute | solution.py:19
  198.6 6.1 copy-start.21
  208.1 6.0 copy-start.24
  217.5 6.0 copy-start.17
  227.0 6.0 copy-start.123
  227.0 11.4 %copy-start.15 = (bf16[192,4,8,256]{3,2,1,0:T(8,128)(2,1)S(1)}, bf16[192,4,8,256]{3,2,1,0:T(8,128)(2,1)}, u32[]{:S(2)}) copy-start(bf16[192,4,8,256]{3,2,1,0:T(8,128)(2,1)} %copy-done.14) | copy-start | bytes 9437188
  235.0 238.3 %collective-permute-start.10 = (f32[64,4,4,128]{3,0,2,1:T(8,128)}, f32[64,4,4,128]{3,0,2,1:T(8,128)}, u32[]{:S(2)}, u32[]{:S(2)}) collective-permute-start(f32[64,4,4,128]{3,0,2,1:T(8,128)} %multiply_add_fusion.1), channel_id=1, source_target_pairs={{0,8},{8,16},{16,24},{1,9},{9,17},{17,25},{2,10},{10,18},{18,26},{... | collective-permute-start | bytes 1572872 | tf_op jit(solution)/shard_map/ppermute | solution.py:27
  247.7 6.0 copy-start.12
  263.0 6.0 copy-start.9
  272.5 6.0 copy-start.7
  322.5 4.3 copy-start.71
  322.5 4.3 copy-start.72
  322.5 4.3 copy-start.73
  340.0 2.9 copy-start.61
  340.0 2.9 copy-start.92
  340.0 2.9 copy-start.121
  345.3 3.5 copy-start.34
  345.3 2.3 copy-start.1
  345.3 3.0 copy-start.36
  349.6 43.9 %collective-permute-start.7 = (bf16[64,1,8,256]{3,2,1,0:T(8,128)(2,1)}, bf16[64,1,8,256]{3,2,1,0:T(8,128)(2,1)S(1)}, u32[]{:S(2)}, u32[]{:S(2)}) collective-permute-start(bf16[64,1,8,256]{3,2,1,0:T(8,128)(2,1)} %get-tuple-element.165), channel_id=1, source_target_pairs={{0,1},{1,2},{2,3},{3,4},{4,5},{5,6},{6,7},{8,9},{9,10},{10,11},{11... | collective-permute-start | bytes 786440 | tf_op jit(solution)/shard_map/ppermute | solution.py:18
  353.6 39.9 %collective-permute-start.8 = (bf16[64,1,8,256]{3,2,1,0:T(8,128)(2,1)}, bf16[64,1,8,256]{3,2,1,0:T(8,128)(2,1)}, u32[]{:S(2)}, u32[]{:S(2)}) collective-permute-start(bf16[64,1,8,256]{3,2,1,0:T(8,128)(2,1)} %get-tuple-element.166), channel_id=1, source_target_pairs={{1,0},{2,1},{3,2},{4,3},{5,4},{6,5},{7,6},{9,8},{10,9},{11,10},{12... | collective-permute-start | bytes 786440 | tf_op jit(solution)/shard_map/ppermute | solution.py:19
  358.8 4.0 copy-start.57
  464.9 144.2 %collective-permute-start.9 = (f32[64,4,4,128]{3,0,2,1:T(8,128)}, f32[64,4,4,128]{3,0,2,1:T(8,128)}, u32[]{:S(2)}, u32[]{:S(2)}) collective-permute-start(f32[64,4,4,128]{3,0,2,1:T(8,128)} %copy.76), channel_id=1, source_target_pairs={{0,8},{8,16},{16,24},{1,9},{9,17},{17,25},{2,10},{10,18},{18,26},{... | collective-permute-start | bytes 1572872 | tf_op jit(solution)/shard_map/ppermute | solution.py:27
  470.7 3.9 copy-start.122
  613.3 16.2 %collective-permute-start = (f32[64,4,4,128]{3,2,1,0:T(4,128)S(1)}, f32[64,4,4,128]{3,2,1,0:T(4,128)S(1)}, u32[]{:S(2)}, u32[]{:S(2)}) collective-permute-start(f32[64,4,4,128]{3,2,1,0:T(4,128)S(1)} %get-tuple-element.235), channel_id=1, source_target_pairs={{0,8},{8,16},{16,24},{1,9},{9,17},{17,25},{2,10},{10,18},{18,26},{... | collective-permute-start | bytes 1572872 | tf_op jit(solution)/shard_map/while/body/eval_jaxpr/ppermute | solution.py:27
  629.6 15.3 %collective-permute-start = (f32[64,4,4,128]{3,2,1,0:T(4,128)S(1)}, f32[64,4,4,128]{3,2,1,0:T(4,128)S(1)}, u32[]{:S(2)}, u32[]{:S(2)}) collective-permute-start(f32[64,4,4,128]{3,2,1,0:T(4,128)S(1)} %get-tuple-element.235), channel_id=1, source_target_pairs={{0,8},{8,16},{16,24},{1,9},{9,17},{17,25},{2,10},{10,18},{18,26},{... | collective-permute-start | bytes 1572872 | tf_op jit(solution)/shard_map/while/body/eval_jaxpr/ppermute | solution.py:27
  645.0 14.4 %collective-permute-start = (f32[64,4,4,128]{3,2,1,0:T(4,128)S(1)}, f32[64,4,4,128]{3,2,1,0:T(4,128)S(1)}, u32[]{:S(2)}, u32[]{:S(2)}) collective-permute-start(f32[64,4,4,128]{3,2,1,0:T(4,128)S(1)} %get-tuple-element.235), channel_id=1, source_target_pairs={{0,8},{8,16},{16,24},{1,9},{9,17},{17,25},{2,10},{10,18},{18,26},{... | collective-permute-start | bytes 1572872 | tf_op jit(solution)/shard_map/while/body/eval_jaxpr/ppermute | solution.py:27
  (74 other events, 131.4 us)
Sparse Core Ops, SparseCore 0:
  473.4 133.4 all-reduce.5
where the time goes:
time: 689 us; the launch traced here: 677 us
  local copies, waits for them, and re-layouts  303 us (44%)
  waiting for transfers between devices  125 us (18%)
  other arithmetic  81.4 us (12%)
  matrix products  73.9 us (11%)
  blocking collectives  45.5 us (7%)
  starting transfers between devices  32.1 us (5%)
  between operations  16.5 us (2%)
    unnamed x292, local copies, waits for them, and re-layouts  129 us
    dot_general x18, local copies, waits for them, and re-layouts, taps_grad(): lax.dot_general(flattened, columns(widened, z_shift, x_shift, planes), ((...  87.3 us
    psum x1, waiting for transfers between devices, on_device(): lax.psum((weight_grad, bias_grad), ('tm', 'slab'))  86.3 us
    slice x8, local copies, waits for them, and re-layouts, columns(): widened[:, z_shift:z_shift + planes, x_shift:x_shift + extent_x, y_shift:...  50.2 us
    psum x1, blocking collectives, on_device(): lax.psum((weight_grad, bias_grad), ('tm', 'slab'))  45.5 us
    ppermute x5, waiting for transfers between devices, passed_along(): lax.ppermute(value, axis, [(source, source + steps) for source in range(i...  38.7 us
    dot_general x36, matrix products, apply_taps(): jnp.dot(matrix, columns(widened, z_shift, x_shift, planes), preferred_ele...  38.6 us
    dot_general x18, matrix products, taps_grad(): lax.dot_general(flattened, columns(widened, z_shift, x_shift, planes), ((...  35.3 us
  transfers between devices with their start and end apart: 14, of which 4 were waited for; matrix products, arithmetic and copies ran while one was open for 43% of the time, Pallas kernels for 0%

commit v1 on v0

v1 whole, which is shorter than its diff:
```python
import functools
import math

import jax
import jax.numpy as jnp
from jax import lax
from jax.experimental import pallas as pl
from jax.experimental.pallas import tpu as pltpu
from jax.sharding import PartitionSpec as P

step_size = 0.25
MESH = pl.DeviceIdType.MESH
f32 = jnp.float32
bf16 = jnp.bfloat16


def banded(taps):
    channels = taps.shape[1]
    ordered = taps.reshape(3, 3, 3, channels, channels).transpose(0, 2, 3, 1, 4)
    rows = ordered.reshape(3, 3, channels, 3 * channels)
    upper = jnp.pad(rows, ((0, 0), (0, 0), (0, 0), (0, channels)))
    lower = jnp.pad(rows, ((0, 0), (0, 0), (0, 0), (channels, 0)))
    return jnp.concatenate([upper, lower], 2).reshape(9, 2 * channels, 4 * channels)


def kernel(
    n_tm, n_slab, chunk,
    u_ref, lam_ref, wf_ref, wb_ref, bias_ref, diag_ref, down_ref, up_ref,
    new_ref, grad_ref,
    v0, v1, g1, g0, halo, sens0, mid, gacc, bacc,
    early, late, early_in, late_in, gsend, rs_in, tm_all, total,
    halo_send, halo_recv, early_send, early_recv, late_send, late_recv,
    rs_send, rs_recv, tm_send, tm_recv, ag_send, ag_recv,
):
    planes, rows, cells = u_ref.shape
    channels = rows // 8
    pair = 2 * channels
    pairs = rows // pair
    me_tm = lax.axis_index("tm")
    me = lax.axis_index("slab")

    def slab_peer(d):
        return lax.rem(me + d, n_slab)

    def tm_peer(d):
        return lax.rem(me_tm + d, n_tm)

    barrier = pltpu.get_barrier_semaphore()
    for d in range(1, n_slab):
        pl.semaphore_signal(barrier, inc=1, device_id={"slab": slab_peer(d)}, device_id_type=MESH)
    for d in range(1, n_tm):
        pl.semaphore_signal(barrier, inc=1, device_id={"tm": tm_peer(d)}, device_id_type=MESH)

    lane = lax.broadcasted_iota(jnp.int32, (pair, cells), 1)

    def put(buf, z, j, value):
        at = pl.ds(pl.multiple_of(channels + j * pair, channels), pair)
        wide = value.astype(f32)
        buf[1, z, at, :] = value
        buf[0, z, at, :] = jnp.where(lane == 0, 0.0, pltpu.roll(wide, 1, 1)).astype(bf16)
        buf[2, z, at, :] = jnp.where(lane == cells - 1, 0.0, pltpu.roll(wide, cells - 1, 1)).astype(bf16)

    def group(j):
        return pl.ds(pl.multiple_of(j * pair, pair), pair)

    def exchange(e, buf, start):
        own = pl.ds(channels, rows)

        def up():
            return pltpu.make_async_remote_copy(
                src_ref=buf.at[1, planes, own], dst_ref=halo.at[e, 0],
                send_sem=halo_send.at[e, 0], recv_sem=halo_recv.at[e, 0],
                device_id={"slab": jnp.minimum(me + 1, n_slab - 1)}, device_id_type=MESH)

        def down():
            return pltpu.make_async_remote_copy(
                src_ref=buf.at[1, 1, own], dst_ref=halo.at[e, 1],
                send_sem=halo_send.at[e, 1], recv_sem=halo_recv.at[e, 1],
                device_id={"slab": jnp.maximum(me - 1, 0)}, device_id_type=MESH)

        if start:
            @pl.when(me < n_slab - 1)
            def _():
                up().start()

            @pl.when(me > 0)
            def _():
                down().start()
        else:
            @pl.when(me > 0)
            def _():
                up().wait_recv()

                def move(j, carry):
                    put(buf, 0, j, halo[e, 0, group(j), :])
                    return carry
                lax.fori_loop(0, pairs, move, 0)

            @pl.when(me == 0)
            def _():
                buf[:, 0, :, :] = jnp.zeros_like(buf[:, 0, :, :])

            @pl.when(me < n_slab - 1)
            def _():
                down().wait_recv()

                def move(j, carry):
                    put(buf, planes + 1, j, halo[e, 1, group(j), :])
                    return carry
                lax.fori_loop(0, pairs, move, 0)

            @pl.when(me == n_slab - 1)
            def _():
                buf[:, planes + 1, :, :] = jnp.zeros_like(buf[:, planes + 1, :, :])

            @pl.when(me < n_slab - 1)
            def _():
                up().wait_send()

            @pl.when(me > 0)
            def _():
                down().wait_send()

    def conv(buf, taps, first, stride, count, finish):
        def body(k, carry):
            z = first + (k // pairs) * stride
            j = lax.rem(k, pairs)
            window = pl.ds(pl.multiple_of(j * pair, pair), 2 * pair)
            acc = jnp.zeros((pair, cells), f32)
            for a in range(3):
                for c in range(3):
                    acc = acc + jnp.dot(taps[3 * a + c], buf[c, z + a, window, :],
                                        preferred_element_type=f32)
            finish(z, j, acc)
            return carry
        lax.fori_loop(0, count * pairs, body, 0)

    def inner(buf, taps, finish):
        if planes > 2:
            conv(buf, taps, 1, 1, planes - 2, finish)

    def outer(buf, taps, finish):
        conv(buf, taps, 0, planes - 1, 2, finish)

    def taps_grad(cot, buf):
        for a in range(3):
            for c in range(3):
                def body(k, carry, a=a, c=c):
                    j = k
                    window = pl.ds(pl.multiple_of(j * pair, pair), 2 * pair)
                    at = pl.ds(pl.multiple_of(channels + j * pair, channels), pair)
                    acc = gacc[3 * a + c]
                    for z in range(planes):
                        acc = acc + lax.dot_general(
                            cot[1, z + 1, at, :], buf[c, z + a, window, :],
                            (((1,), (1,)), ((), ())), preferred_element_type=f32)
                    gacc[3 * a + c] = acc
                    return carry
                lax.fori_loop(0, pairs, body, 0)

    def restricted(value):
        summed = (value[:channels] + value[channels:]).astype(bf16)
        return jnp.dot(summed, down_ref[...], preferred_element_type=f32)

    def half(j):
        return pl.ds(pl.multiple_of(j * channels, channels), channels)

    def load_u(k, carry):
        j = lax.rem(k, pairs)
        z = k // pairs
        put(v0, z + 1, j, u_ref[z, group(j), :])
        return carry
    lax.fori_loop(0, planes * pairs, load_u, 0)

    pl.semaphore_wait(barrier, n_slab - 1 + n_tm - 1)
    exchange(0, v0, True)

    for buf in (v0, v1, g1, g0):
        for c in range(3):
            for z in range(planes + 2):
                buf[c, z, :channels, :] = jnp.zeros((channels, cells), bf16)
                buf[c, z, channels + rows:, :] = jnp.zeros((channels, cells), bf16)
    gacc[...] = jnp.zeros_like(gacc)
    bacc[...] = jnp.zeros_like(bacc)

    def after_first(z, j, acc):
        th = jnp.tanh(acc + bias_ref[...])
        sens = 1.0 - th * th
        sens0[z, group(j), :] = sens
        state = (u_ref[z, group(j), :].astype(f32) + step_size * th).astype(bf16)
        put(v1, z + 1, j, state)
        early[0, z, half(j), :] = (1.0 + 2.0 * step_size * diag_ref[...] * restricted(sens)).astype(bf16)
        early[1, z, half(j), :] = restricted(lam_ref[z, group(j), :]).astype(bf16)

    inner(v0, wf_ref, after_first)
    exchange(0, v0, False)
    outer(v0, wf_ref, after_first)
    exchange(1, v1, True)

    def to_later(src, dst, send, recv, d):
        return pltpu.make_async_remote_copy(
            src_ref=src, dst_ref=dst.at[d - 1], send_sem=send.at[d - 1], recv_sem=recv.at[d - 1],
            device_id={"tm": jnp.minimum(me_tm + d, n_tm - 1)}, device_id_type=MESH)

    for d in range(1, n_tm):
        @pl.when(me_tm + d < n_tm)
        def _(d=d):
            to_later(early, early_in, early_send, early_recv, d).start()

    def after_second(z, j, acc):
        th = jnp.tanh(acc + bias_ref[...])
        cot = ((1.0 - th * th) * lam_ref[z, group(j), :]).astype(bf16)
        bacc[...] += cot.astype(f32)
        put(g1, z + 1, j, cot)

    inner(v1, wf_ref, after_second)
    exchange(1, v1, False)
    outer(v1, wf_ref, after_second)
    exchange(2, g1, True)
    taps_grad(g1, v1)

    def after_third(z, j, acc):
        middle = lam_ref[z, group(j), :] + step_size * acc
        mid[z, group(j), :] = middle
        cot = (sens0[z, group(j), :] * middle).astype(bf16)
        bacc[...] += cot.astype(f32)
        put(g0, z + 1, j, cot)

    inner(g1, wb_ref, after_third)
    exchange(2, g1, False)
    outer(g1, wb_ref, after_third)
    exchange(3, g0, True)
    taps_grad(g0, v0)

    three = 3 * channels
    for t in range(9):
        block = gacc[t, :channels, :three] + gacc[t, channels:, channels:]
        gsend[t * channels:(t + 1) * channels, :three] = block.astype(bf16)
        side = jnp.zeros((channels, channels), f32)
        if t == 0:
            column = jnp.sum(bacc[:channels] + bacc[channels:], axis=1, keepdims=True)
            side = side + column
        gsend[t * channels:(t + 1) * channels, three:] = side.astype(bf16)
    padding = n_slab * chunk - 9 * channels
    if padding:
        gsend[9 * channels:, :] = jnp.zeros((padding, 4 * channels), bf16)

    def part(index):
        return pl.ds(pl.multiple_of(index * chunk, 16), chunk)

    def scatter(d):
        return pltpu.make_async_remote_copy(
            src_ref=gsend.at[part(slab_peer(d))], dst_ref=rs_in.at[d - 1],
            send_sem=rs_send.at[d - 1], recv_sem=rs_recv.at[d - 1],
            device_id={"slab": slab_peer(d)}, device_id_type=MESH)

    for d in range(1, n_slab):
        scatter(d).start()

    def after_fourth(z, j, acc):
        back = mid[z, group(j), :] + step_size * acc
        late[z, half(j), :] = restricted(back).astype(bf16)

    inner(g0, wb_ref, after_fourth)
    exchange(3, g0, False)
    outer(g0, wb_ref, after_fourth)

    for d in range(1, n_tm):
        @pl.when(me_tm + d < n_tm)
        def _(d=d):
            to_later(late, late_in, late_send, late_recv, d).start()

    mine = gsend[part(me), :].astype(f32)
    for d in range(1, n_slab):
        scatter(d).wait_recv()
        mine = mine + rs_in[d - 1].astype(f32)
    tm_all[me_tm] = mine.astype(bf16)

    def across(d):
        return pltpu.make_async_remote_copy(
            src_ref=tm_all.at[me_tm], dst_ref=tm_all.at[me_tm],
            send_sem=tm_send.at[d - 1], recv_sem=tm_recv.at[d - 1],
            device_id={"tm": tm_peer(d)}, device_id_type=MESH)

    for d in range(1, n_tm):
        across(d).start()
    for d in range(1, n_tm):
        across(d).wait_recv()
    whole = tm_all[0].astype(f32)
    for k in range(1, n_tm):
        whole = whole + tm_all[k].astype(f32)
    total[me] = whole.astype(bf16)

    def spread(d):
        return pltpu.make_async_remote_copy(
            src_ref=total.at[me], dst_ref=total.at[me],
            send_sem=ag_send.at[d - 1], recv_sem=ag_recv.at[d - 1],
            device_id={"slab": slab_peer(d)}, device_id_type=MESH)

    for d in range(1, n_slab):
        spread(d).start()

    for d in range(1, n_tm):
        @pl.when(me_tm >= d)
        def _(d=d):
            to_later(early, early_in, early_send, early_recv, d).wait_recv()
            to_later(late, late_in, late_send, late_recv, d).wait_recv()

    for d in range(n_tm):
        @pl.when(me_tm == d)
        def _(d=d):
            def body(k, carry):
                z = k // pairs
                j = lax.rem(k, pairs)
                at = half(j)
                first = early if d == 0 else early_in.at[d - 1]
                value = -first[1, z, at, :].astype(f32)
                for s in range(d, 0, -1):
                    lam_next = (early if s == 1 else early_in.at[s - 2])[1, z, at, :]
                    value = (early_in[s - 1, 0, z, at, :].astype(f32) * value
                             + late_in[s - 1, z, at, :].astype(f32) - lam_next.astype(f32))
                high = value.astype(bf16)
                low = (value - high.astype(f32)).astype(bf16)
                fine = (jnp.dot(high, up_ref[...], preferred_element_type=f32)
                        + jnp.dot(low, up_ref[...], preferred_element_type=f32))
                new_ref[z, group(j), :] = lam_ref[z, group(j), :] + jnp.concatenate([fine, fine], 0)
                return carry
            lax.fori_loop(0, planes * pairs, body, 0)

    for d in range(1, n_slab):
        spread(d).wait_recv()
    for s in range(n_slab):
        grad_ref[s] = total[s].astype(f32)

    for d in range(1, n_slab):
        scatter(d).wait_send()
        spread(d).wait_send()
    for d in range(1, n_tm):
        across(d).wait_send()

        @pl.when(me_tm + d < n_tm)
        def _(d=d):
            to_later(early, early_in, early_send, early_recv, d).wait_send()
            to_later(late, late_in, late_send, late_recv, d).wait_send()


def on_device(u_states, lam_points, weight, bias):
    n_tm, n_slab = lax.axis_size("tm"), lax.axis_size("slab")
    _, channels, planes, extent_x, cells = u_states.shape
    rows = channels * extent_x
    chunk = 16 * -(-9 * channels // (16 * n_slab))
    state = u_states[0].transpose(1, 2, 0, 3).reshape(planes, rows, cells)
    adjoint = lam_points[0].transpose(1, 2, 0, 3).reshape(planes, rows, cells)
    forward = banded(weight)
    backward = banded(weight[::-1].transpose(0, 2, 1))
    offset = jnp.tile(bias, 2)[:, None]
    diagonal = jnp.diagonal(weight[13]).astype(f32)[:, None]
    fine = lax.broadcasted_iota(jnp.int32, (cells, cells // 2), 0) // 2
    coarse = lax.broadcasted_iota(jnp.int32, (cells, cells // 2), 1)
    chosen = fine == coarse
    down = jnp.where(chosen, 0.25, 0.0).astype(bf16)
    up = jnp.where(chosen, 1.0, 0.0).astype(bf16).T
    wide = pltpu.VMEM((3, planes + 2, rows + 2 * channels, cells), bf16)
    small = (planes, rows // 2, cells // 2)
    dma = pltpu.SemaphoreType.DMA
    updated, grads = pl.pallas_call(
        functools.partial(kernel, n_tm, n_slab, chunk),
        out_shape=(
            jax.ShapeDtypeStruct((planes, rows, cells), f32),
            jax.ShapeDtypeStruct((n_slab, chunk, 4 * channels), f32),
        ),
        in_specs=[pl.BlockSpec(memory_space=pltpu.VMEM)] * 8,
        out_specs=[pl.BlockSpec(memory_space=pltpu.VMEM)] * 2,
        scratch_shapes=[
            wide, wide, wide, wide,
            pltpu.VMEM((4, 2, rows, cells), bf16),
            pltpu.VMEM((planes, rows, cells), f32),
            pltpu.VMEM((planes, rows, cells), f32),
            pltpu.VMEM((9, 2 * channels, 4 * channels), f32),
            pltpu.VMEM((2 * channels, cells), f32),
            pltpu.VMEM((2,) + small, bf16),
            pltpu.VMEM(small, bf16),
            pltpu.VMEM((n_tm - 1, 2) + small, bf16),
            pltpu.VMEM((n_tm - 1,) + small, bf16),
            pltpu.VMEM((n_slab * chunk, 4 * channels), bf16),
            pltpu.VMEM((n_slab - 1, chunk, 4 * channels), bf16),
            pltpu.VMEM((n_tm, chunk, 4 * channels), bf16),
            pltpu.VMEM((n_slab, chunk, 4 * channels), bf16),
            dma((4, 2)), dma((4, 2)),
            dma((n_tm - 1,)), dma((n_tm - 1,)), dma((n_tm - 1,)), dma((n_tm - 1,)),
            dma((n_slab - 1,)), dma((n_slab - 1,)),
            dma((n_tm - 1,)), dma((n_tm - 1,)),
            dma((n_slab - 1,)), dma((n_slab - 1,)),
        ],
        compiler_params=pltpu.CompilerParams(
            collective_id=0, has_side_effects=True, vmem_limit_bytes=56 * 2**20
        ),
        cost_estimate=pl.CostEstimate(flops=15 * 10**9, bytes_accessed=8 * 10**6, transcendentals=10**6),
    )(state, adjoint, forward, backward, offset, diagonal, down, up)
    lam_new = updated.reshape(planes, extent_x, channels, cells).transpose(2, 0, 1, 3)
    scale = step_size / math.sqrt(2 * n_tm * planes * n_slab * extent_x * cells)
    flat = grads.reshape(n_slab * chunk, 4 * channels)[: 9 * channels] * scale
    taps = flat[:, : 3 * channels].reshape(3, 3, channels, 3, channels)
    grad_w = taps.transpose(0, 3, 1, 2, 4).reshape(27, channels, channels)
    grad_b = flat[:channels, 3 * channels]
    return (lam_new[None], grad_w, grad_b)


def solution(mesh):
    in_specs = (P("tm", None, "slab", None, None), P("tm", None, "slab", None, None), P(), P())
    out_specs = (P("tm", None, "slab", None, None), P(), P())
    return jax.shard_map(
        on_device, mesh=mesh, in_specs=in_specs, out_specs=out_specs, check_vma=False
    )
```

time: 689 us -> 108 us (0.16)
  the two profiles are of different devices: /device:TPU:4 before, /device:TPU:29 now
where the time goes in v1:
time: 108 us
  Pallas kernels  86.7 us (80%)
  local copies, waits for them, and re-layouts  18.3 us (17%)
  other arithmetic  2.15 us (2%)
    pallas_call x1, Pallas kernels, on_device(): pl.pallas_call(functools.partial(kernel, n_tm, n_slab, chunk), out_shape=...  86.7 us
    reshape x1, local copies, waits for them, and re-layouts, on_device(): updated.reshape(planes, extent_x, channels, cells).transpose(2, 0, 1, 3)  4.19 us
    transpose x1, local copies, waits for them, and re-layouts, on_device(): adjoint = lam_points[0].transpose(1, 2, 0, 3).reshape(planes, rows, cells)  2.53 us

profile of v1, /device:TPU:29, one launch (start us, length us, event | category | flops | bytes accessed | tf_op | source)
XLA Modules:
  0.0 107.9 jit_solution(236126163063077176)
XLA Ops:
  0.7 0.7 tile.2
  1.3 0.7 slice_bitcast_fusion
  2.0 0.9 gather_fusion
  2.9 0.7 copy.33.diag_ref
  3.6 0.8 broadcast_in_dim_tile.4.bias_ref
  4.4 0.8 select_convert_fusion.1.down_ref
  5.2 0.6 select_convert_fusion.up_ref
  5.8 1.3 %copy.28 = bf16[3,3,3,64,64]{3,4,1,2,0:T(8,128)(2,1)S(1)} copy(bf16[3,3,3,64,64]{4,3,2,1,0:T(8,128)(2,1)} %bitcast.45) | data formatting | bytes 442368 | tf_op jit(solution)/shard_map/reshape | solution.py:19
  7.1 0.0 copy-start.1
  7.1 0.3 fusion.4
  7.4 1.1 copy.29
  8.5 0.0 copy-done.1
  8.6 0.0 copy-start.2
  8.6 0.3 fusion.5
  8.9 1.1 copy.31
  10.0 0.0 copy-start
  10.0 0.0 copy-done.2
  10.0 1.6 %copy.26 = bf16[4,8,64,256]{3,2,1,0:T(8,128)(2,1)} copy(bf16[4,8,64,256]{3,1,0,2:T(8,128)(2,1)S(1)} %bitcast.49) | data formatting | bytes 2097152 | tf_op jit(solution)/shard_map/transpose | solution.py:352
  11.5 0.1 copy-done
  11.6 2.5 %copy.27 = f32[4,8,64,256]{3,2,1,0:T(8,128)} copy(f32[4,8,64,256]{3,1,0,2:T(8,128)S(1)} %bitcast.41) | data formatting | bytes 4194304 | tf_op jit(solution)/shard_map/transpose | solution.py:353
  14.2 86.7 %shard_map.67 = (f32[4,512,256]{2,1,0:T(8,128)}, f32[8,80,256]{2,1,0:T(8,128)}) custom-call(bf16[4,512,256]{2,1,0:T(8,128)(2,1)} %bitcast.50, f32[4,512,256]{2,1,0:T(8,128)} %bitcast.44, bf16[9,128,256]{2,1,0:T(8,128)(2,1)} %bitcast.52, bf16[9,128,256]{2,1,0:T(8,128)(2,1)} %bitcast.53, f32[128,1]{1,0:T(8,128)} %broadcast_in_dim_tile.4.bias_ref, ...), custom_call_target="tpu_custom_call" | custom-call | flops 15000000512 | bytes 8000000 | tf_op jit(solution)/shard_map/pallas_call | solution.py:366
  100.9 0.0 copy-start.3
  100.9 4.2 %copy.39 = f32[4,8,64,256]{3,1,0,2:T(8,128)} copy(f32[4,8,64,256]{3,2,1,0:T(8,128)} %bitcast.43) | data formatting | bytes 4194304 | tf_op jit(solution)/shard_map/reshape | solution.py:400
  105.1 0.0 copy-done.3
  105.1 0.2 copy.37
  105.4 0.1 broadcast_multiply_fusion
  105.4 0.5 slice_bitcast_fusion.1
  106.0 0.5 reshape.62
  106.5 1.4 %copy.36 = f32[3,3,3,64,64]{4,3,2,1,0:T(8,128)} copy(f32[3,3,3,64,64]{3,2,0,4,1:T(4,128)S(1)} %bitcast.40) | data formatting | bytes 884736 | tf_op jit(solution)/shard_map/transpose | solution.py:404
  (8 shorter events, 0.2 us)
Async XLA Ops:
  7.1 1.4 %copy-start.1 = (bf16[27,64,64]{2,1,0:T(8,128)(2,1)S(1)}, bf16[27,64,64]{2,1,0:T(8,128)(2,1)}, u32[]{:S(2)}) copy-start(bf16[27,64,64]{2,1,0:T(8,128)(2,1)} %param.6) | copy-start | bytes 663556
  8.6 1.4 %copy-start.2 = (bf16[1,64,4,8,256]{4,3,2,1,0:T(8,128)(2,1)S(1)}, bf16[1,64,4,8,256]{4,3,2,1,0:T(8,128)(2,1)}, u32[]{:S(2)}) copy-start(bf16[1,64,4,8,256]{4,3,2,1,0:T(8,128)(2,1)} %param.4) | copy-start | bytes 3145732
  10.0 1.7 %copy-start = (f32[1,64,4,8,256]{4,3,2,1,0:T(8,128)S(1)}, f32[1,64,4,8,256]{4,3,2,1,0:T(8,128)}, u32[]{:S(2)}) copy-start(f32[1,64,4,8,256]{4,3,2,1,0:T(8,128)} %param.5) | copy-start | bytes 6291460
  100.9 4.2 %copy-start.3 = (f32[8,80,256]{2,1,0:T(8,128)S(1)}, f32[8,80,256]{2,1,0:T(8,128)}, u32[]{:S(2)}) copy-start(f32[8,80,256]{2,1,0:T(8,128)} %get-tuple-element.6) | copy-start | bytes 1966084

commit v2 on v1

--- a/solution.py
+++ b/solution.py
@@ -14,19 +14,11 @@
 bf16 = jnp.bfloat16
 
 
-def banded(taps):
-    channels = taps.shape[1]
-    ordered = taps.reshape(3, 3, 3, channels, channels).transpose(0, 2, 3, 1, 4)
-    rows = ordered.reshape(3, 3, channels, 3 * channels)
-    upper = jnp.pad(rows, ((0, 0), (0, 0), (0, 0), (0, channels)))
-    lower = jnp.pad(rows, ((0, 0), (0, 0), (0, 0), (channels, 0)))
-    return jnp.concatenate([upper, lower], 2).reshape(9, 2 * channels, 4 * channels)
-
-
 def kernel(
     n_tm, n_slab, chunk,
-    u_ref, lam_ref, wf_ref, wb_ref, bias_ref, diag_ref, down_ref, up_ref,
+    u_ref, lam_ref, weight_ref, bias_ref,
     new_ref, grad_ref,
+    wf_ref, wb_ref, down_ref, up_ref, partial,
     v0, v1, g1, g0, halo, sens0, mid, gacc, bacc,
     early, late, early_in, late_in, gsend, rs_in, tm_all, total,
     halo_send, halo_recv, early_send, early_recv, late_send, late_recv,
@@ -121,42 +113,60 @@
             def _():
                 down().wait_send()
 
-    def conv(buf, taps, first, stride, count, finish):
-        def body(k, carry):
-            z = first + (k // pairs) * stride
-            j = lax.rem(k, pairs)
-            window = pl.ds(pl.multiple_of(j * pair, pair), 2 * pair)
-            acc = jnp.zeros((pair, cells), f32)
-            for a in range(3):
+    def window(j):
+        return pl.ds(pl.multiple_of(j * pair, pair), 2 * pair)
+
+    def inner(buf, taps, finish):
+        def body(j, carry):
+            acc = [None] * planes
+            for source in range(1, planes + 1):
+                used = [a for a in range(3) if 0 <= source - a < planes]
+                low, high = used[0] * pair, (used[-1] + 1) * pair
+                out = None
                 for c in range(3):
-                    acc = acc + jnp.dot(taps[3 * a + c], buf[c, z + a, window, :],
-                                        preferred_element_type=f32)
-            finish(z, j, acc)
+                    product = jnp.dot(taps[c, low:high, :], buf[c, source, window(j), :],
+                                      preferred_element_type=f32)
+                    out = product if out is None else out + product
+                for n, a in enumerate(used):
+                    piece = out[n * pair:(n + 1) * pair]
+                    z = source - a
+                    acc[z] = piece if acc[z] is None else acc[z] + piece
+                done = source - 2
+                if 0 < done < planes - 1:
+                    finish(done, j, acc[done])
+            partial[0, group(j), :] = acc[0]
+            partial[1, group(j), :] = acc[planes - 1]
             return carry
-        lax.fori_loop(0, count * pairs, body, 0)
-
-    def inner(buf, taps, finish):
-        if planes > 2:
-            conv(buf, taps, 1, 1, planes - 2, finish)
+        lax.fori_loop(0, pairs, body, 0)
 
     def outer(buf, taps, finish):
-        conv(buf, taps, 0, planes - 1, 2, finish)
+        def body(j, carry):
+            for n, (source, a) in enumerate(((0, 0), (planes + 1, 2))):
+                acc = partial[n, group(j), :]
+                for c in range(3):
+                    acc = acc + jnp.dot(taps[c, a * pair:(a + 1) * pair, :],
+                                        buf[c, source, window(j), :], preferred_element_type=f32)
+                finish(source - a, j, acc)
+            return carry
+        lax.fori_loop(0, pairs, body, 0)
 
     def taps_grad(cot, buf):
-        for a in range(3):
+        def body(j, carry):
+            at = pl.ds(pl.multiple_of(channels + j * pair, channels), pair)
             for c in range(3):
-                def body(k, carry, a=a, c=c):
-                    j = k
-                    window = pl.ds(pl.multiple_of(j * pair, pair), 2 * pair)
-                    at = pl.ds(pl.multiple_of(channels + j * pair, channels), pair)
-                    acc = gacc[3 * a + c]
-                    for z in range(planes):
-                        acc = acc + lax.dot_general(
-                            cot[1, z + 1, at, :], buf[c, z + a, window, :],
-                            (((1,), (1,)), ((), ())), preferred_element_type=f32)
-                    gacc[3 * a + c] = acc
-                    return carry
-                lax.fori_loop(0, pairs, body, 0)
+                acc = [None] * 3
+                for source in range(planes + 2):
+                    used = [a for a in range(3) if 0 <= source - a < planes]
+                    left = jnp.concatenate([cot[1, source - a + 1, at, :] for a in used], 0)
+                    out = lax.dot_general(left, buf[c, source, window(j), :],
+                                          (((1,), (1,)), ((), ())), preferred_element_type=f32)
+                    for n, a in enumerate(used):
+                        piece = out[n * pair:(n + 1) * pair]
+                        acc[a] = piece if acc[a] is None else acc[a] + piece
+                for a in range(3):
+                    gacc[3 * a + c] += acc[a]
+            return carry
+        lax.fori_loop(0, pairs, body, 0)
 
     def restricted(value):
         summed = (value[:channels] + value[channels:]).astype(bf16)
@@ -172,8 +182,36 @@
         return carry
     lax.fori_loop(0, planes * pairs, load_u, 0)
 
+    def place(taps, a, b, c, block):
+        taps[c, a * pair:a * pair + channels, b * channels:(b + 1) * channels] = block
+        taps[c, a * pair + channels:(a + 1) * pair, (b + 1) * channels:(b + 2) * channels] = block
+
+    wf_ref[...] = jnp.zeros_like(wf_ref)
+    for a in range(3):
+        for b in range(3):
+            for c in range(3):
+                place(wf_ref, a, b, c, weight_ref[9 * a + 3 * b + c])
+
     pl.semaphore_wait(barrier, n_slab - 1 + n_tm - 1)
     exchange(0, v0, True)
+
+    wb_ref[...] = jnp.zeros_like(wb_ref)
+    for a in range(3):
+        for b in range(3):
+            for c in range(3):
+                block = weight_ref[26 - (9 * a + 3 * b + c)].astype(f32)
+                place(wb_ref, a, b, c, block.T.astype(bf16))
+    fine_at = lax.broadcasted_iota(jnp.int32, (cells, cells // 2), 0) // 2
+    coarse_at = lax.broadcasted_iota(jnp.int32, (cells, cells // 2), 1)
+    down_ref[...] = jnp.where(fine_at == coarse_at, 0.25, 0.0).astype(bf16)
+    fine_at = lax.broadcasted_iota(jnp.int32, (cells // 2, cells), 1) // 2
+    coarse_at = lax.broadcasted_iota(jnp.int32, (cells // 2, cells), 0)
+    up_ref[...] = jnp.where(fine_at == coarse_at, 1.0, 0.0).astype(bf16)
+    row = lax.rem(lax.broadcasted_iota(jnp.int32, (pair, channels), 0), channels)
+    column_at = lax.broadcasted_iota(jnp.int32, (pair, channels), 1)
+    offset = jnp.sum(jnp.where(row == column_at, bias_ref[...], 0.0), axis=1, keepdims=True)
+    middle_tap = weight_ref[13].astype(f32)
+    diagonal = jnp.sum(jnp.where((row == column_at)[:channels], middle_tap, 0.0), axis=1, keepdims=True)
 
     for buf in (v0, v1, g1, g0):
         for c in range(3):
@@ -184,12 +222,12 @@
     bacc[...] = jnp.zeros_like(bacc)
 
     def after_first(z, j, acc):
-        th = jnp.tanh(acc + bias_ref[...])
+        th = jnp.tanh(acc + offset)
         sens = 1.0 - th * th
         sens0[z, group(j), :] = sens
         state = (u_ref[z, group(j), :].astype(f32) + step_size * th).astype(bf16)
         put(v1, z + 1, j, state)
-        early[0, z, half(j), :] = (1.0 + 2.0 * step_size * diag_ref[...] * restricted(sens)).astype(bf16)
+        early[0, z, half(j), :] = (1.0 + 2.0 * step_size * diagonal * restricted(sens)).astype(bf16)
         early[1, z, half(j), :] = restricted(lam_ref[z, group(j), :]).astype(bf16)
 
     inner(v0, wf_ref, after_first)
@@ -208,7 +246,7 @@
             to_later(early, early_in, early_send, early_recv, d).start()
 
     def after_second(z, j, acc):
-        th = jnp.tanh(acc + bias_ref[...])
+        th = jnp.tanh(acc + offset)
         cot = ((1.0 - th * th) * lam_ref[z, group(j), :]).astype(bf16)
         bacc[...] += cot.astype(f32)
         put(g1, z + 1, j, cot)
@@ -351,15 +389,6 @@
     chunk = 16 * -(-9 * channels // (16 * n_slab))
     state = u_states[0].transpose(1, 2, 0, 3).reshape(planes, rows, cells)
     adjoint = lam_points[0].transpose(1, 2, 0, 3).reshape(planes, rows, cells)
-    forward = banded(weight)
-    backward = banded(weight[::-1].transpose(0, 2, 1))
-    offset = jnp.tile(bias, 2)[:, None]
-    diagonal = jnp.diagonal(weight[13]).astype(f32)[:, None]
-    fine = lax.broadcasted_iota(jnp.int32, (cells, cells // 2), 0) // 2
-    coarse = lax.broadcasted_iota(jnp.int32, (cells, cells // 2), 1)
-    chosen = fine == coarse
-    down = jnp.where(chosen, 0.25, 0.0).astype(bf16)
-    up = jnp.where(chosen, 1.0, 0.0).astype(bf16).T
     wide = pltpu.VMEM((3, planes + 2, rows + 2 * channels, cells), bf16)
     small = (planes, rows // 2, cells // 2)
     dma = pltpu.SemaphoreType.DMA
@@ -369,9 +398,14 @@
             jax.ShapeDtypeStruct((planes, rows, cells), f32),
             jax.ShapeDtypeStruct((n_slab, chunk, 4 * channels), f32),
         ),
-        in_specs=[pl.BlockSpec(memory_space=pltpu.VMEM)] * 8,
+        in_specs=[pl.BlockSpec(memory_space=pltpu.VMEM)] * 4,
         out_specs=[pl.BlockSpec(memory_space=pltpu.VMEM)] * 2,
         scratch_shapes=[
+            pltpu.VMEM((3, 6 * channels, 4 * channels), bf16),
+            pltpu.VMEM((3, 6 * channels, 4 * channels), bf16),
+            pltpu.VMEM((cells, cells // 2), bf16),
+            pltpu.VMEM((cells // 2, cells), bf16),
+            pltpu.VMEM((2, rows, cells), f32),
             wide, wide, wide, wide,
             pltpu.VMEM((4, 2, rows, cells), bf16),
             pltpu.VMEM((planes, rows, cells), f32),
@@ -396,7 +430,7 @@
             collective_id=0, has_side_effects=True, vmem_limit_bytes=56 * 2**20
         ),
         cost_estimate=pl.CostEstimate(flops=15 * 10**9, bytes_accessed=8 * 10**6, transcendentals=10**6),
-    )(state, adjoint, forward, backward, offset, diagonal, down, up)
+    )(state, adjoint, weight, bias[None])
     lam_new = updated.reshape(planes, extent_x, channels, cells).transpose(2, 0, 1, 3)
     scale = step_size / math.sqrt(2 * n_tm * planes * n_slab * extent_x * cells)
     flat = grads.reshape(n_slab * chunk, 4 * channels)[: 9 * channels] * scale

time: 108 us -> 78.2 us (0.72)
  Pallas kernels: 86.7 us -> 64.8 us
  local copies, waits for them, and re-layouts: 18.3 us -> 12.4 us
  other arithmetic: 2.15 us -> 0.06 us
    pallas_call x1, Pallas kernels: 86.7 us -> 64.8 us  [on_device(): pl.pallas_call(functools.partial(kernel, n_tm, n_slab, chunk), out_shape=...]
    concatenate x2 -> x0, local copies, waits for them, and re-layouts: 2.14 us -> none  [banded(): jnp.concatenate([upper, lower], 2).reshape(9, 2 * channels, 4 * channels)]
    convert_element_type x3 -> x0, other arithmetic: 1.43 us -> none  [the longest x1 0.79 us: on_device(): down = jnp.where(chosen, 0.25, 0.0).astype(bf16)]
    another operation x2 -> x0, local copies, waits for them, and re-layouts: 1.42 us -> none  [on_device(): offset = jnp.tile(bias, 2)[:, None]]
    transpose x1, local copies, waits for them, and re-layouts: 1.57 us -> 2.96 us  [on_device(): state = u_states[0].transpose(1, 2, 0, 3).reshape(planes, rows, cells)]
    reshape x2 -> x0, local copies, waits for them, and re-layouts: 1.29 us -> none  [banded(): ordered = taps.reshape(3, 3, 3, channels, channels).transpose(0, 2, 3, 1, 4)]
where the time goes in v2:
time: 78.2 us; the launch traced here: 78 us
  Pallas kernels  64.8 us (83%)
  local copies, waits for them, and re-layouts  12.4 us (16%)
    pallas_call x1, Pallas kernels, on_device(): pl.pallas_call(functools.partial(kernel, n_tm, n_slab, chunk), out_shape=...  64.8 us
    reshape x1, local copies, waits for them, and re-layouts, on_device(): updated.reshape(planes, extent_x, channels, cells).transpose(2, 0, 1, 3)  4.19 us
    transpose x1, local copies, waits for them, and re-layouts, on_device(): state = u_states[0].transpose(1, 2, 0, 3).reshape(planes, rows, cells)  2.96 us
    transpose x1, local copies, waits for them, and re-layouts, on_device(): adjoint = lam_points[0].transpose(1, 2, 0, 3).reshape(planes, rows, cells)  2.54 us

profile of v2, /device:TPU:29, one launch (start us, length us, event | category | flops | bytes accessed | tf_op | source)
XLA Modules:
  0.0 78.0 jit_solution(8906733451068966871)
XLA Ops:
  0.6 0.0 copy-start
  0.6 3.0 %copy.16 = bf16[4,8,64,256]{3,2,1,0:T(8,128)(2,1)} copy(bf16[4,8,64,256]{3,1,0,2:T(8,128)(2,1)} %bitcast.27) | data formatting | bytes 2097152 | tf_op jit(solution)/shard_map/transpose | solution.py:390
  3.6 0.0 copy-done
  3.6 2.5 %copy.17 = f32[4,8,64,256]{3,2,1,0:T(8,128)} copy(f32[4,8,64,256]{3,1,0,2:T(8,128)S(1)} %bitcast.23) | data formatting | bytes 4194304 | tf_op jit(solution)/shard_map/transpose | solution.py:391
  6.1 64.8 %shard_map.67 = (f32[4,512,256]{2,1,0:T(8,128)}, f32[8,80,256]{2,1,0:T(8,128)}) custom-call(bf16[4,512,256]{2,1,0:T(8,128)(2,1)} %bitcast.28, f32[4,512,256]{2,1,0:T(8,128)} %bitcast.26, bf16[27,64,64]{2,1,0:T(8,128)(2,1)} %weight_ref.1, f32[1,64]{1,0:T(1,128)} %bitcast.31), custom_call_target="tpu_custom_call" | custom-call | flops 15000000512 | bytes 8000000 | tf_op jit(solution)/shard_map/pallas_call | solution.py:395
  71.0 0.0 copy-start.1
  71.0 4.2 %copy.23 = f32[4,8,64,256]{3,1,0,2:T(8,128)} copy(f32[4,8,64,256]{3,2,1,0:T(8,128)} %bitcast.25) | data formatting | bytes 4194304 | tf_op jit(solution)/shard_map/reshape | solution.py:434
  75.2 0.0 copy-done.1
  75.2 0.2 copy.21
  75.5 0.1 broadcast_multiply_fusion
  75.5 0.5 slice_bitcast_fusion
  76.1 0.5 reshape.28
  76.6 1.4 %copy.20 = f32[3,3,3,64,64]{4,3,2,1,0:T(8,128)} copy(f32[3,3,3,64,64]{3,2,0,4,1:T(4,128)S(1)} %bitcast.22) | data formatting | bytes 884736 | tf_op jit(solution)/shard_map/transpose | solution.py:438
  (2 shorter events, 0.1 us)
Async XLA Ops:
  0.6 3.0 %copy-start = (f32[1,64,4,8,256]{4,3,2,1,0:T(8,128)S(1)}, f32[1,64,4,8,256]{4,3,2,1,0:T(8,128)}, u32[]{:S(2)}) copy-start(f32[1,64,4,8,256]{4,3,2,1,0:T(8,128)} %param.5) | copy-start | bytes 6291460
  71.0 4.2 %copy-start.1 = (f32[8,80,256]{2,1,0:T(8,128)S(1)}, f32[8,80,256]{2,1,0:T(8,128)}, u32[]{:S(2)}) copy-start(f32[8,80,256]{2,1,0:T(8,128)} %get-tuple-element.6) | copy-start | bytes 1966084

commit v3 on v2

--- a/solution.py
+++ b/solution.py
@@ -15,9 +15,10 @@
 
 
 def kernel(
-    n_tm, n_slab, chunk,
-    u_ref, lam_ref, weight_ref, bias_ref,
-    new_ref, grad_ref,
+    n_tm, n_slab, chunk, scale,
+    u_ref, lam_hbm, weight_ref, bias_ref,
+    new_hbm, grad_ref, gbias_ref,
+    lam_ref, new_ref, lam_sem, new_sem,
     wf_ref, wb_ref, down_ref, up_ref, partial,
     v0, v1, g1, g0, halo, sens0, mid, gacc, bacc,
     early, late, early_in, late_in, gsend, rs_in, tm_all, total,
@@ -30,6 +31,18 @@
     pairs = rows // pair
     me_tm = lax.axis_index("tm")
     me = lax.axis_index("slab")
+
+    def lam_copy(z, x):
+        return pltpu.make_async_copy(
+            lam_hbm.at[0, :, z, x, :], lam_ref.at[z, pl.ds(x * channels, channels), :], lam_sem.at[z, x])
+
+    def new_copy(z, x):
+        return pltpu.make_async_copy(
+            new_ref.at[z, pl.ds(x * channels, channels), :], new_hbm.at[0, :, z, x, :], new_sem.at[z, x])
+
+    everywhere = [(z, x) for z in range(planes) for x in range(8)]
+    for z, x in everywhere:
+        lam_copy(z, x).start()
 
     def slab_peer(d):
         return lax.rem(me + d, n_slab)
@@ -230,6 +243,8 @@
         early[0, z, half(j), :] = (1.0 + 2.0 * step_size * diagonal * restricted(sens)).astype(bf16)
         early[1, z, half(j), :] = restricted(lam_ref[z, group(j), :]).astype(bf16)
 
+    for z, x in everywhere:
+        lam_copy(z, x).wait()
     inner(v0, wf_ref, after_first)
     exchange(0, v0, False)
     outer(v0, wf_ref, after_first)
@@ -365,10 +380,19 @@
                 return carry
             lax.fori_loop(0, planes * pairs, body, 0)
 
+    for z, x in everywhere:
+        new_copy(z, x).start()
     for d in range(1, n_slab):
         spread(d).wait_recv()
-    for s in range(n_slab):
-        grad_ref[s] = total[s].astype(f32)
+    summed = total[...].astype(f32).reshape(n_slab * chunk, 4 * channels) * scale
+    for a in range(3):
+        for c in range(3):
+            t = 3 * a + c
+            for b in range(3):
+                grad_ref[9 * a + 3 * b + c] = summed[t * channels:(t + 1) * channels,
+                                                     b * channels:(b + 1) * channels]
+    gbias_ref[...] = jnp.sum(
+        jnp.where((row == column_at)[:channels], summed[:channels, three:], 0.0), axis=0, keepdims=True)
 
     for d in range(1, n_slab):
         scatter(d).wait_send()
@@ -380,6 +404,8 @@
         def _(d=d):
             to_later(early, early_in, early_send, early_recv, d).wait_send()
             to_later(late, late_in, late_send, late_recv, d).wait_send()
+    for z, x in everywhere:
+        new_copy(z, x).wait()
 
 
 def on_device(u_states, lam_points, weight, bias):
@@ -388,19 +414,29 @@
     rows = channels * extent_x
     chunk = 16 * -(-9 * channels // (16 * n_slab))
     state = u_states[0].transpose(1, 2, 0, 3).reshape(planes, rows, cells)
-    adjoint = lam_points[0].transpose(1, 2, 0, 3).reshape(planes, rows, cells)
+    scale = step_size / math.sqrt(2 * n_tm * planes * n_slab * extent_x * cells)
     wide = pltpu.VMEM((3, planes + 2, rows + 2 * channels, cells), bf16)
     small = (planes, rows // 2, cells // 2)
     dma = pltpu.SemaphoreType.DMA
-    updated, grads = pl.pallas_call(
-        functools.partial(kernel, n_tm, n_slab, chunk),
+    lam_new, grad_w, grad_b = pl.pallas_call(
+        functools.partial(kernel, n_tm, n_slab, chunk, scale),
         out_shape=(
-            jax.ShapeDtypeStruct((planes, rows, cells), f32),
-            jax.ShapeDtypeStruct((n_slab, chunk, 4 * channels), f32),
+            jax.ShapeDtypeStruct(lam_points.shape, f32),
+            jax.ShapeDtypeStruct((27, channels, channels), f32),
+            jax.ShapeDtypeStruct((1, channels), f32),
         ),
-        in_specs=[pl.BlockSpec(memory_space=pltpu.VMEM)] * 4,
-        out_specs=[pl.BlockSpec(memory_space=pltpu.VMEM)] * 2,
+        in_specs=[
+            pl.BlockSpec(memory_space=pltpu.VMEM), pl.BlockSpec(memory_space=pl.ANY),
+            pl.BlockSpec(memory_space=pltpu.VMEM), pl.BlockSpec(memory_space=pltpu.VMEM),
+        ],
+        out_specs=[
+            pl.BlockSpec(memory_space=pl.ANY),
+            pl.BlockSpec(memory_space=pltpu.VMEM), pl.BlockSpec(memory_space=pltpu.VMEM),
+        ],
         scratch_shapes=[
+            pltpu.VMEM((planes, rows, cells), f32),
+            pltpu.VMEM((planes, rows, cells), f32),
+            dma((planes, extent_x)), dma((planes, extent_x)),
             pltpu.VMEM((3, 6 * channels, 4 * channels), bf16),
             pltpu.VMEM((3, 6 * channels, 4 * channels), bf16),
             pltpu.VMEM((cells, cells // 2), bf16),
@@ -430,14 +466,8 @@
             collective_id=0, has_side_effects=True, vmem_limit_bytes=56 * 2**20
         ),
         cost_estimate=pl.CostEstimate(flops=15 * 10**9, bytes_accessed=8 * 10**6, transcendentals=10**6),
-    )(state, adjoint, weight, bias[None])
-    lam_new = updated.reshape(planes, extent_x, channels, cells).transpose(2, 0, 1, 3)
-    scale = step_size / math.sqrt(2 * n_tm * planes * n_slab * extent_x * cells)
-    flat = grads.reshape(n_slab * chunk, 4 * channels)[: 9 * channels] * scale
-    taps = flat[:, : 3 * channels].reshape(3, 3, channels, 3, channels)
-    grad_w = taps.transpose(0, 3, 1, 2, 4).reshape(27, channels, channels)
-    grad_b = flat[:channels, 3 * channels]
-    return (lam_new[None], grad_w, grad_b)
+    )(state, lam_points, weight, bias[None])
+    return (lam_new, grad_w, grad_b[0])
 
 
 def solution(mesh):

time: 78.2 us -> 72.8 us (0.931)
  local copies, waits for them, and re-layouts: 12.4 us -> 7.44 us
    reshape x2 -> x0, local copies, waits for them, and re-layouts: 4.71 us -> none  [the longest x1 4.19 us: on_device(): updated.reshape(planes, extent_x, channels, cells).transpose(2, 0, 1, 3)]
    unnamed x5 -> x7, local copies, waits for them, and re-layouts: 0.24 us -> 4.67 us
    transpose x2 -> x0, local copies, waits for them, and re-layouts: 3.95 us -> none  [the longest x1 2.54 us: on_device(): adjoint = lam_points[0].transpose(1, 2, 0, 3).reshape(planes, rows, cells)]
where the time goes in v3:
time: 72.8 us; the launch traced here: 72.6 us
  Pallas kernels  64.5 us (89%)
  local copies, waits for them, and re-layouts  7.44 us (10%)
    pallas_call x1, Pallas kernels, on_device(): pl.pallas_call(functools.partial(kernel, n_tm, n_slab, chunk, scale), out...  64.5 us
    unnamed x7, local copies, waits for them, and re-layouts  4.67 us
    transpose x1, local copies, waits for them, and re-layouts, on_device(): state = u_states[0].transpose(1, 2, 0, 3).reshape(planes, rows, cells)  2.78 us

profile of v3, /device:TPU:29, one launch (start us, length us, event | category | flops | bytes accessed | tf_op | source)
XLA Modules:
  0.0 72.6 jit_solution(7251706497290776140)
XLA Ops:
  0.6 2.8 %copy.7 = bf16[4,8,64,256]{3,2,1,0:T(8,128)(2,1)} copy(bf16[4,8,64,256]{3,1,0,2:T(8,128)(2,1)} %bitcast.6) | data formatting | bytes 2097152 | tf_op jit(solution)/shard_map/transpose | solution.py:416
  3.4 64.5 %shard_map.67 = (f32[1,64,4,8,256]{4,3,2,1,0:T(8,128)}, f32[27,64,64]{2,1,0:T(8,128)}, f32[1,64]{1,0:T(1,128)}) custom-call(bf16[4,512,256]{2,1,0:T(8,128)(2,1)} %bitcast.7, f32[1,64,4,8,256]{4,3,2,1,0:T(8,128)} %lam_hbm.1, bf16[27,64,64]{2,1,0:T(8,128)(2,1)} %weight_ref.1, f32[1,64]{1,0:T(1,128)} %bitcast.8), custom_call_target="tpu_custom_call" | custom-call | flops 15000000512 | bytes 8000000 | tf_op jit(solution)/shard_map/pallas_call | solution.py:421
  67.9 0.0 copy-start
  67.9 0.0 copy-start.1
  67.9 3.2 %copy.11 = f32[1,64,4,8,256]{4,3,2,1,0:T(8,128)} copy(f32[1,64,4,8,256]{4,3,2,1,0:T(8,128)} %get-tuple-element.12) | data formatting | bytes 4194304
  71.2 0.0 copy-done
  71.2 0.9 %copy.12 = f32[27,64,64]{2,1,0:T(8,128)} copy(f32[27,64,64]{2,1,0:T(8,128)S(1)} %copy-done) | data formatting | bytes 884736
  72.1 0.0 copy-done.1
  72.1 0.5 copy.13
Async XLA Ops:
  67.9 3.3 %copy-start = (f32[27,64,64]{2,1,0:T(8,128)S(1)}, f32[27,64,64]{2,1,0:T(8,128)}, u32[]{:S(2)}) copy-start(f32[27,64,64]{2,1,0:T(8,128)} %get-tuple-element.13) | copy-start | bytes 1327108
  67.9 4.2 %copy-start.1 = (f32[1,64]{1,0:T(1,128)S(1)}, f32[1,64]{1,0:T(1,128)}, u32[]{:S(2)}) copy-start(f32[1,64]{1,0:T(1,128)} %get-tuple-element.8) | copy-start | bytes 772
